TPU v7x, 512 devices: a whole 4x4x16 slice. The times are simulated.
512 devices in a mesh: wide: 32 (over z, core), narrow: 16 (over x, y).
Axes of the slice: x: 4, y: 4, z: 16, core: 2. Of those that a mesh axis runs over, the one named last changes fastest.
Arguments:
- activations: bfloat16 [512, 16384], P(None, 'wide'), may hold values from -6 to 6
- enc_weight: bfloat16 [16384, 16384], P('wide', 'narrow'), may hold values from -0.046875 to 0.046875
- enc_bias: float32 [16384], P('narrow'), may hold values from -4 to 4
- dec_weight: bfloat16 [16384, 16384], P('narrow', 'wide'), may hold values from -0.375 to 0.375
- dec_bias: float32 [16384], P('wide'), may hold values from -4 to 4
- active_ids: int32 [512, 64], replicated, may hold values from 0 to 16383, all different within a row
Outputs:
- dec_grad: bfloat16 [16384, 16384], P('narrow', 'wide')
- latent_grad: float32 [512, 16384], P('wide', 'narrow')
Inputs may be any that keep to these rules, and one draw needn't show every extreme that they name: `active_ids`: each row names 64 different latents; every latent is named by some row.
All inputs are finite; a program needn't handle non-finite values.
Results may differ from a plain program's by a relative error of at most 0.0058.
Values may be sent and summed in bfloat16 or wider, within the bound.
No kernel may reach another device: no remote copies, remote signals or barrier semaphores. Data moves between devices by JAX's collectives and lax.ppermute only.
A program may use at most 128 MiB of HBM per device.

v0:
```python
import jax
import jax.numpy as jnp
from jax import lax
from jax.sharding import Mesh
from jax.sharding import PartitionSpec as P

NARROW = ("narrow_0", "narrow_1")
WIDE = ("wide_0", "wide_1")


def filled_with(value, identity):
    return jnp.broadcast_to(jnp.asarray(identity, value.dtype), value.shape)


def carried_in(value, axes, combine, identity, reverse):
    before = start = filled_with(value, identity)
    total = value
    for axis in reversed(axes):
        length, position = (lax.axis_size(axis), lax.axis_index(axis))
        pieces = lax.all_gather(total, axis)
        inside, total = (start, start)
        for k in reversed(range(length)) if reverse else range(length):
            passed = k > position if reverse else k < position
            total = combine(total, pieces[k])
            inside = jnp.where(passed, total, inside)
        before = combine(inside, before)
    return before


def reduced_to_own(pieces, axes, turns):
    inside = pieces.shape[1:]
    pieces = pieces.reshape(*(lax.axis_size(a) for a in axes), *inside)
    pieces = jnp.moveaxis(pieces, turns, range(len(axes))).reshape(-1, *inside)
    for k in turns:
        pieces = lax.psum_scatter(pieces, axes[k], scatter_dimension=0, tiled=True)
    return pieces[0]


def in_blocks(value, dim, length):
    dims = value.shape
    pieces = value.reshape(*dims[:dim], length, dims[dim] // length, *dims[dim + 1 :])
    return jnp.moveaxis(pieces, dim, 0)


def summed_rows(value, axes, turns, dim):
    length = lax.axis_size(axes)
    return reduced_to_own(in_blocks(value, dim, length), axes, turns)


def add_fields(earlier, later):
    return jax.tree.map(jnp.add, earlier, later)


def local(activations, enc_weight, enc_bias, dec_weight, dec_bias, active_ids):
    token_count = activations.shape[0]
    latent_width = enc_weight.shape[1]
    groups = lax.axis_size(NARROW)
    group_index = lax.axis_index(NARROW)
    first_latent = group_index * latent_width
    inside = (active_ids >= first_latent) & (active_ids < first_latent + latent_width)
    local_ids = jnp.where(inside, active_ids - first_latent, latent_width)
    row_index = jnp.arange(token_count, dtype=jnp.int32)[:, None]
    active_mask = (
        jnp.zeros((token_count, latent_width), jnp.float32)
        .at[row_index, local_ids]
        .set(1.0, mode="drop")
    )
    share_rows = token_count // lax.axis_size(WIDE)
    offset = lax.axis_index(WIDE) * share_rows
    own_mask = lax.dynamic_slice_in_dim(active_mask, offset, share_rows, 0)
    partial_pre = jnp.dot(activations, enc_weight, preferred_element_type=jnp.float32)
    preact = lax.psum(partial_pre, WIDE) + enc_bias
    latents = (active_mask * preact).astype(jnp.bfloat16)
    recon_part = jnp.dot(latents, dec_weight, preferred_element_type=jnp.float32)
    target = activations.astype(jnp.float32)
    nothing = jnp.zeros_like(recon_part)
    before = carried_in(recon_part, NARROW, add_fields, nothing, False)
    errors_here = dec_bias + before + recon_part - target
    later_sum = carried_in(errors_here, NARROW, add_fields, nothing, True)
    suffix = later_sum + errors_here
    errors = (suffix / groups).astype(jnp.bfloat16)
    dec_grad = lax.dot_general(
        latents, errors, (((0,), (0,)), ((), ())), preferred_element_type=jnp.float32
    ).astype(jnp.bfloat16)
    latent_rows = summed_rows(
        lax.dot_general(
            errors, dec_weight, (((1,), (1,)), ((), ())), preferred_element_type=jnp.float32
        ),
        WIDE,
        (1, 0),
        0,
    )
    latent_out = own_mask * latent_rows
    return (dec_grad, latent_out)


def solution(mesh):
    split = Mesh(mesh.devices.reshape(16, 2, 4, 4), ("wide_0", "wide_1", "narrow_0", "narrow_1"))
    return jax.shard_map(
        local,
        mesh=split,
        in_specs=(P(None, WIDE), P(WIDE, NARROW), P(NARROW), P(NARROW, WIDE), P(WIDE), P()),
        out_specs=(P(NARROW, WIDE), P(WIDE, NARROW)),
        check_vma=False,
    )
```

profile of v0, /device:TPU:2, one launch (start us, length us, event | category | flops | bytes accessed | tf_op | source)
XLA Modules:
  0.0 583.1 jit_solution(8263159260602203690)
XLA Ops:
  7.2 0.0 copy-start
  7.2 0.0 copy-start.7
  7.2 0.0 all-reduce.2.cloned.1.call-start
  7.2 3.5 fusion.17
  10.8 0.0 copy-start.11
  10.8 0.0 copy-start.10
  10.8 0.0 all-reduce.2.cloned.1.call-update
  10.8 0.0 all-gather.11.cloned.1.call-start
  10.8 0.0 copy-done.7
  10.9 0.5 copy-done.11
  11.4 0.1 multiply_reduce_fusion
  11.5 0.0 copy-done.10
  11.5 0.1 and_reduce_fusion
  11.7 0.1 copy.10
  11.8 0.1 reshape.66
  11.9 121.5 %scatter_custom_fusion = f32[524288]{0:T(1024)} fusion(s32[32768]{0:T(1024)S(1)} %reshape.66, f32[32768]{0:T(1024)S(1)} %broadcast.52, f32[]{:T(128)} %constant.17.clone.1), kind=kCustom, calls=%fused_computation.31 | custom fusion | bytes 2097156
  133.4 0.0 copy-start.8
  133.4 1.7 reshape.63
  135.1 0.0 copy-start.2
  135.1 94.1 %all-reduce.2.cloned.1.call-done = f32[512,1024]{1,0:T(8,128)} async-done(((f32[512,1024]{1,0:T(8,128)}), f32[512,1024]{1,0:T(8,128)}) %all-reduce.2.cloned.1.call-update) | async-done | bytes 2097168 | tf_op jit(solution)/shard_map/psum | solution.py:72
  229.2 0.0 copy-done.8
  229.2 2.1 multiply_convert_fusion
  231.3 0.0 copy-done.2
  231.3 0.0 copy-start.5
  231.3 1.0 copy-done.5
  232.3 0.0 copy-done
  232.3 1.7 fusion.18
  234.0 0.0 all-gather.11.cloned.1.call-update
  234.0 0.0 copy-start.3
  234.0 0.0 copy-start.4
  234.0 0.0 copy-start.9
  234.0 0.0 all-gather.7.cloned.1.call-start
  234.1 56.1 %all-gather.11.cloned.1.call-done = f32[2048,512]{1,0:T(8,128)} async-done(((f32[512,512]{1,0:T(8,128)}), f32[2048,512]{1,0:T(8,128)}) %all-gather.11.cloned.1.call-update) | async-done | bytes 4194320 | tf_op jit(solution)/shard_map/all_gather | solution.py:20
  290.1 3.7 fusion.13
  293.8 0.0 all-gather.7.cloned.1.call-update
  293.8 0.0 all-gather.13.cloned.1.call-start
  293.9 55.8 %all-gather.7.cloned.1.call-done = f32[4,512,512]{2,1,0:T(8,128)} async-done(((f32[1,512,512]{2,1,0:T(8,128)}), f32[4,512,512]{2,1,0:T(8,128)}) %all-gather.7.cloned.1.call-update) | async-done | bytes 4194320 | tf_op jit(solution)/shard_map/all_gather | solution.py:20
  349.7 0.0 copy-done.3
  349.7 0.0 copy-done.4
  349.7 0.0 copy-done.9
  349.7 5.6 fusion.12
  355.3 0.0 all-gather.13.cloned.1.call-update
  355.3 0.0 copy-start.1
  355.3 0.0 all-gather.9.cloned.1.call-start
  355.4 57.1 %all-gather.13.cloned.1.call-done = f32[2048,512]{1,0:T(8,128)} async-done(((f32[512,512]{1,0:T(8,128)}), f32[2048,512]{1,0:T(8,128)}) %all-gather.13.cloned.1.call-update) | async-done | bytes 4194320 | tf_op jit(solution)/shard_map/all_gather | solution.py:20
  412.5 3.7 fusion.6
  416.1 0.0 all-gather.9.cloned.1.call-update
  416.2 0.0 reduce-scatter.3.cloned.1.call-start
  416.2 55.8 %all-gather.9.cloned.1.call-done = f32[4,512,512]{2,1,0:T(8,128)} async-done(((f32[1,512,512]{2,1,0:T(8,128)}), f32[4,512,512]{2,1,0:T(8,128)}) %all-gather.9.cloned.1.call-update) | async-done | bytes 4194320 | tf_op jit(solution)/shard_map/all_gather | solution.py:20
  472.0 0.0 copy-done.1
  472.0 4.6 fusion.5
  476.6 0.7 fusion.19
  477.4 1.5 copy.11
  478.8 0.0 copy-start.6
  478.8 0.0 reduce-scatter.3.cloned.1.call-update
  478.9 0.0 reduce-scatter.5.cloned.1.call-start
  478.9 21.2 %reduce-scatter.3.cloned.1.call-done = f32[16,16,1024]{2,1,0:T(8,128)} async-done(((f32[32,16,1024]{2,1,0:T(8,128)}), f32[16,16,1024]{2,1,0:T(8,128)}) %reduce-scatter.3.cloned.1.call-update) | async-done | bytes 1048592 | tf_op jit(solution)/shard_map/reduce_scatter | solution.py:35
  500.1 0.0 reduce-scatter.5.cloned.1.call-update
  500.2 0.0 copy-done.6
  500.2 1.7 convolution_convert_fusion
  501.9 72.8 %reduce-scatter.5.cloned.1.call-done = f32[1,16,1024]{2,1,0:T(8,128)} async-done(((f32[16,16,1024]{2,1,0:T(8,128)}), f32[1,16,1024]{2,1,0:T(8,128)}) %reduce-scatter.5.cloned.1.call-update) | async-done | bytes 65552 | tf_op jit(solution)/shard_map/reduce_scatter | solution.py:35
  574.7 1.5 bitcast_multiply_fusion
  (4 shorter events, 0.1 us)
Async XLA Ops:
  7.2 225.1 %copy-start = (bf16[1024,512]{1,0:T(8,128)(2,1)S(1)}, bf16[1024,512]{1,0:T(8,128)(2,1)}, u32[]{:S(2)}) copy-start(bf16[1024,512]{1,0:T(8,128)(2,1)} %param.9) | copy-start | bytes 3145732
  7.2 3.7 copy-start.7
  7.2 222.0 %all-reduce.2.cloned.1.call-start = ((), (), s32[]{:S(2)}) async-start(), calls=%async_computation.2 | async-start | bytes 4194304 | tf_op jit(solution)/shard_map/psum | solution.py:72
  10.8 0.7 copy-start.11
  10.8 0.7 copy-start.10
  10.8 279.3 %all-gather.11.cloned.1.call-start = ((), (), s32[]{:S(2)}) async-start(), calls=%async_computation.7 | async-start | bytes 5242880 | tf_op jit(solution)/shard_map/all_gather | solution.py:20
  133.4 95.8 %copy-start.8 = (f32[1024]{0:T(1024)S(1)}, f32[1024]{0:T(1024)}, u32[]{:S(2)}) copy-start(f32[1024]{0:T(1024)} %param.8) | copy-start | bytes 12292
  135.1 96.2 %copy-start.2 = (f32[512,1024]{1,0:T(8,128)}, f32[512,1024]{1,0:T(8,128)S(1)}, u32[]{:S(2)}) copy-start(f32[512,1024]{1,0:T(8,128)S(1)} %reshape.63) | copy-start | bytes 6291460
  231.3 1.0 copy-start.5
  234.0 115.7 %copy-start.3 = (f32[512,512]{1,0:T(8,128)S(1)}, f32[512,512]{1,0:T(8,128)}, u32[]{:S(2)}) copy-start(f32[512,512]{1,0:T(8,128)} %fusion.18) | copy-start | bytes 3145732
  234.0 115.7 %copy-start.4 = (bf16[512,512]{1,0:T(8,128)(2,1)S(1)}, bf16[512,512]{1,0:T(8,128)(2,1)}, u32[]{:S(2)}) copy-start(bf16[512,512]{1,0:T(8,128)(2,1)} %param.6) | copy-start | bytes 1572868
  234.0 115.7 %copy-start.9 = (f32[512]{0:T(512)S(1)}, f32[512]{0:T(512)}, u32[]{:S(2)}) copy-start(f32[512]{0:T(512)} %param.10) | copy-start | bytes 6148
  234.0 115.6 %all-gather.7.cloned.1.call-start = ((), (), s32[]{:S(2)}) async-start(), calls=%async_computation.3 | async-start | bytes 5242880 | tf_op jit(solution)/shard_map/all_gather | solution.py:20
  293.8 118.7 %all-gather.13.cloned.1.call-start = ((), (), s32[]{:S(2)}) async-start(), calls=%async_computation.8 | async-start | bytes 5242880 | tf_op jit(solution)/shard_map/all_gather | solution.py:20
  355.3 116.7 %copy-start.1 = (f32[512,512]{1,0:T(8,128)S(1)}, f32[512,512]{1,0:T(8,128)}, u32[]{:S(2)}) copy-start(f32[512,512]{1,0:T(8,128)} %fusion.12) | copy-start | bytes 3145732
  355.3 116.7 %all-gather.9.cloned.1.call-start = ((), (), s32[]{:S(2)}) async-start(), calls=%async_computation.4 | async-start | bytes 5242880 | tf_op jit(solution)/shard_map/all_gather | solution.py:20
  416.2 84.0 %reduce-scatter.3.cloned.1.call-start = ((), (), s32[]{:S(2)}) async-start(), calls=%async_computation.5 | async-start | bytes 3145728 | tf_op jit(solution)/shard_map/reduce_scatter | solution.py:35
  478.8 21.3 %copy-start.6 = (bf16[512,1024]{1,0:T(8,128)(2,1)S(1)}, bf16[512,1024]{1,0:T(8,128)(2,1)}, u32[]{:S(2)}) copy-start(bf16[512,1024]{1,0:T(8,128)(2,1)} %copy-done.5) | copy-start | bytes 3145732
  478.9 95.9 %reduce-scatter.5.cloned.1.call-start = ((), (), s32[]{:S(2)}) async-start(), calls=%async_computation.6 | async-start | bytes 1114112 | tf_op jit(solution)/shard_map/reduce_scatter | solution.py:35
Sparse Core Ops, SparseCore 0:
  10.9 218.2 all-reduce.1
  234.1 55.9 all-gather.10
  293.9 55.6 all-gather.6
  355.4 57.0 all-gather.12
  416.3 55.6 all-gather.8
  479.0 21.1 reduce-scatter.2
  502.9 71.7 reduce-scatter.4
where the time goes:
time: 583 us
  waiting for transfers between devices  413 us (71%)
  local copies, waits for them, and re-layouts  126 us (22%)
  other arithmetic  21.4 us (4%)
  between operations  14.3 us (2%)
  matrix products  7.66 us (1%)
    all_gather x4, waiting for transfers between devices, carried_in(): pieces = lax.all_gather(total, axis)  225 us
    unnamed x28, local copies, waits for them, and re-layouts  123 us
    reduce_scatter x2, waiting for transfers between devices, reduced_to_own(): pieces = lax.psum_scatter(pieces, axes[k], scatter_dimension=0, tiled=True)  94.1 us
    psum x1, waiting for transfers between devices, local(): preact = lax.psum(partial_pre, WIDE) + enc_bias  94.1 us
  transfers between devices with their start and end apart: 7, of which 7 were waited for; matrix products, arithmetic and copies ran while one was open for 22% of the time, Pallas kernels for 0%

commit v1 on v0

--- a/solution.py
+++ b/solution.py
@@ -69,7 +69,7 @@
     offset = lax.axis_index(WIDE) * share_rows
     own_mask = lax.dynamic_slice_in_dim(active_mask, offset, share_rows, 0)
     partial_pre = jnp.dot(activations, enc_weight, preferred_element_type=jnp.float32)
-    preact = lax.psum(partial_pre, WIDE) + enc_bias
+    preact = lax.psum(lax.psum(partial_pre, "wide_1"), "wide_0") + enc_bias
     latents = (active_mask * preact).astype(jnp.bfloat16)
     recon_part = jnp.dot(latents, dec_weight, preferred_element_type=jnp.float32)
     target = activations.astype(jnp.float32)

time: 583 us -> 556 us (0.954)
  waiting for transfers between devices: 413 us -> 386 us
    psum x1 -> x2, waiting for transfers between devices: 94.1 us -> 71.2 us  [local(): preact = lax.psum(lax.psum(partial_pre, 'wide_1'), 'wide_0') + enc_bias]
  transfers between devices with their start and end apart: 7 -> 8, of which waited for: 7 -> 8; matrix products, arithmetic and copies ran while one was open for 22% -> 23% of each run, Pallas kernels for 0% -> 0%
where the time goes in v1:
time: 556 us
  waiting for transfers between devices  386 us (69%)
  local copies, waits for them, and re-layouts  126 us (23%)
  other arithmetic  21.4 us (4%)
  between operations  14.4 us (3%)
  matrix products  7.65 us (1%)
    all_gather x4, waiting for transfers between devices, carried_in(): pieces = lax.all_gather(total, axis)  221 us
    unnamed x28, local copies, waits for them, and re-layouts  123 us
    reduce_scatter x2, waiting for transfers between devices, reduced_to_own(): pieces = lax.psum_scatter(pieces, axes[k], scatter_dimension=0, tiled=True)  94.1 us
    psum x2, waiting for transfers between devices, local(): preact = lax.psum(lax.psum(partial_pre, 'wide_1'), 'wide_0') + enc_bias  71.2 us
  transfers between devices with their start and end apart: 8, of which 8 were waited for; matrix products, arithmetic and copies ran while one was open for 23% of the time, Pallas kernels for 0%

profile of v1, /device:TPU:2, one launch (start us, length us, event | category | flops | bytes accessed | tf_op | source)
XLA Modules:
  0.0 555.7 jit_solution(12931996394928359852)
XLA Ops:
  7.2 0.0 copy-start
  7.2 0.0 all-reduce.3.cloned.1.call-start
  7.2 3.5 fusion.17
  10.7 0.0 copy-start.7
  10.7 0.0 copy-start.11
  10.7 0.0 copy-start.10
  10.7 0.0 all-reduce.3.cloned.1.call-update
  10.8 0.0 all-reduce.5.cloned.1.call-start
  10.8 46.9 %all-reduce.3.cloned.1.call-done = f32[512,1024]{1,0:T(8,128)} async-done(((f32[512,1024]{1,0:T(8,128)}), f32[512,1024]{1,0:T(8,128)}) %all-reduce.3.cloned.1.call-update) | async-done | bytes 2097168 | tf_op jit(solution)/shard_map/psum | solution.py:72
  57.7 0.0 all-reduce.5.cloned.1.call-update
  57.7 0.0 all-gather.11.cloned.1.call-start
  57.8 0.0 copy-done.7
  57.8 0.0 copy-done.11
  57.8 0.1 multiply_reduce_fusion
  57.9 0.0 copy-done.10
  58.0 0.1 and_reduce_fusion
  58.1 0.1 copy.10
  58.2 0.1 reshape.66
  58.4 121.5 %scatter_custom_fusion = f32[524288]{0:T(1024)} fusion(s32[32768]{0:T(1024)S(1)} %reshape.66, f32[32768]{0:T(1024)S(1)} %broadcast.52, f32[]{:T(128)} %constant.17.clone.1), kind=kCustom, calls=%fused_computation.31 | custom fusion | bytes 2097156
  179.8 0.0 copy-start.8
  179.8 1.7 reshape.63
  181.6 0.0 copy-start.2
  181.6 24.3 %all-reduce.5.cloned.1.call-done = f32[512,1024]{1,0:T(8,128)} async-done(((f32[512,1024]{1,0:T(8,128)}), f32[512,1024]{1,0:T(8,128)}) %all-reduce.5.cloned.1.call-update) | async-done | bytes 2097168 | tf_op jit(solution)/shard_map/psum | solution.py:72
  205.9 0.0 copy-done.8
  205.9 2.1 multiply_convert_fusion
  208.0 0.0 copy-done.2
  208.0 0.0 copy-start.5
  208.0 1.0 copy-done.5
  209.0 0.0 copy-done
  209.0 1.7 fusion.18
  210.6 0.0 all-gather.11.cloned.1.call-update
  210.7 0.0 copy-start.3
  210.7 0.0 copy-start.4
  210.7 0.0 copy-start.9
  210.7 0.0 all-gather.7.cloned.1.call-start
  210.8 52.0 %all-gather.11.cloned.1.call-done = f32[2048,512]{1,0:T(8,128)} async-done(((f32[512,512]{1,0:T(8,128)}), f32[2048,512]{1,0:T(8,128)}) %all-gather.11.cloned.1.call-update) | async-done | bytes 4194320 | tf_op jit(solution)/shard_map/all_gather | solution.py:20
  262.8 3.7 fusion.13
  266.4 0.0 all-gather.7.cloned.1.call-update
  266.4 0.0 all-gather.13.cloned.1.call-start
  266.5 55.8 %all-gather.7.cloned.1.call-done = f32[4,512,512]{2,1,0:T(8,128)} async-done(((f32[1,512,512]{2,1,0:T(8,128)}), f32[4,512,512]{2,1,0:T(8,128)}) %all-gather.7.cloned.1.call-update) | async-done | bytes 4194320 | tf_op jit(solution)/shard_map/all_gather | solution.py:20
  322.3 0.0 copy-done.3
  322.3 0.0 copy-done.4
  322.3 0.0 copy-done.9
  322.3 5.6 %fusion.12 = f32[512,512]{1,0:T(8,128)} fusion(f32[512,512]{1,0:T(8,128)S(1)} %copy-done.3, f32[4,512,512]{2,1,0:T(8,128)} %all-gather.7.cloned.1.call-done, bf16[512,512]{1,0:T(8,128)(2,1)S(1)} %copy-done.4, f32[2048,512]{1,0:T(8,128)} %all-gather.11.cloned.1.call-done, f32[512]{0:T(512)S(1)} %copy-done.9, pred[]{:T(512)S(6)} %gt.29, pred[]{:T(512)S(6)} %gt.30, ...), kind=kLoop, calls=%fused_computation.22 | loop fusion | flops 4980736 | bytes 11012104 | tf_op jit(solution)/shard_map/sub | solution.py:78
  327.9 0.0 all-gather.13.cloned.1.call-update
  327.9 0.0 copy-start.1
  327.9 0.0 all-gather.9.cloned.1.call-start
  328.0 57.1 %all-gather.13.cloned.1.call-done = f32[2048,512]{1,0:T(8,128)} async-done(((f32[512,512]{1,0:T(8,128)}), f32[2048,512]{1,0:T(8,128)}) %all-gather.13.cloned.1.call-update) | async-done | bytes 4194320 | tf_op jit(solution)/shard_map/all_gather | solution.py:20
  385.1 3.7 fusion.6
  388.8 0.0 all-gather.9.cloned.1.call-update
  388.8 0.0 reduce-scatter.3.cloned.1.call-start
  388.9 55.8 %all-gather.9.cloned.1.call-done = f32[4,512,512]{2,1,0:T(8,128)} async-done(((f32[1,512,512]{2,1,0:T(8,128)}), f32[4,512,512]{2,1,0:T(8,128)}) %all-gather.9.cloned.1.call-update) | async-done | bytes 4194320 | tf_op jit(solution)/shard_map/all_gather | solution.py:20
  444.6 0.0 copy-done.1
  444.6 4.6 fusion.5
  449.2 0.7 fusion.19
  450.0 1.5 copy.11
  451.5 0.0 reduce-scatter.3.cloned.1.call-update
  451.5 0.0 reduce-scatter.5.cloned.1.call-start
  451.5 21.2 %reduce-scatter.3.cloned.1.call-done = f32[16,16,1024]{2,1,0:T(8,128)} async-done(((f32[32,16,1024]{2,1,0:T(8,128)}), f32[16,16,1024]{2,1,0:T(8,128)}) %reduce-scatter.3.cloned.1.call-update) | async-done | bytes 1048592 | tf_op jit(solution)/shard_map/reduce_scatter | solution.py:35
  472.8 0.0 reduce-scatter.5.cloned.1.call-update
  472.8 0.0 copy-done.6
  472.8 1.7 convolution_convert_fusion
  474.5 72.8 %reduce-scatter.5.cloned.1.call-done = f32[1,16,1024]{2,1,0:T(8,128)} async-done(((f32[16,16,1024]{2,1,0:T(8,128)}), f32[1,16,1024]{2,1,0:T(8,128)}) %reduce-scatter.5.cloned.1.call-update) | async-done | bytes 65552 | tf_op jit(solution)/shard_map/reduce_scatter | solution.py:35
  547.4 1.5 bitcast_multiply_fusion
  (5 shorter events, 0.1 us)
Async XLA Ops:
  7.2 201.8 %copy-start = (bf16[1024,512]{1,0:T(8,128)(2,1)S(1)}, bf16[1024,512]{1,0:T(8,128)(2,1)}, u32[]{:S(2)}) copy-start(bf16[1024,512]{1,0:T(8,128)(2,1)} %param.9) | copy-start | bytes 3145732
  7.2 50.5 %all-reduce.3.cloned.1.call-start = ((), (), s32[]{:S(2)}) async-start(), calls=%async_computation.2 | async-start | bytes 4194304 | tf_op jit(solution)/shard_map/psum | solution.py:72
  10.7 47.0 %copy-start.7 = (s32[512,64]{0,1:T(8,128)S(1)}, s32[512,64]{0,1:T(8,128)}, u32[]{:S(2)}) copy-start(s32[512,64]{0,1:T(8,128)} %param.11) | copy-start | bytes 393220
  10.7 47.1 %copy-start.11 = (s32[2]{0:T(128)S(1)}, s32[2]{0:T(128)}, u32[]{:S(2)}) copy-start(s32[2]{0:T(128)} %constant.47) | copy-start | bytes 28
  10.7 47.2 %copy-start.10 = (s32[2]{0:T(128)S(1)}, s32[2]{0:T(128)}, u32[]{:S(2)}) copy-start(s32[2]{0:T(128)} %constant.50) | copy-start | bytes 28
  10.8 195.1 %all-reduce.5.cloned.1.call-start = ((), (), s32[]{:S(2)}) async-start(), calls=%async_computation.3 | async-start | bytes 4194304 | tf_op jit(solution)/shard_map/psum | solution.py:72
  57.7 205.0 %all-gather.11.cloned.1.call-start = ((), (), s32[]{:S(2)}) async-start(), calls=%async_computation.8 | async-start | bytes 5242880 | tf_op jit(solution)/shard_map/all_gather | solution.py:20
  179.8 26.0 %copy-start.8 = (f32[1024]{0:T(1024)S(1)}, f32[1024]{0:T(1024)}, u32[]{:S(2)}) copy-start(f32[1024]{0:T(1024)} %param.8) | copy-start | bytes 12292
  181.6 26.4 %copy-start.2 = (f32[512,1024]{1,0:T(8,128)}, f32[512,1024]{1,0:T(8,128)S(1)}, u32[]{:S(2)}) copy-start(f32[512,1024]{1,0:T(8,128)S(1)} %reshape.63) | copy-start | bytes 6291460
  208.0 1.0 copy-start.5
  210.7 111.6 %copy-start.3 = (f32[512,512]{1,0:T(8,128)S(1)}, f32[512,512]{1,0:T(8,128)}, u32[]{:S(2)}) copy-start(f32[512,512]{1,0:T(8,128)} %fusion.18) | copy-start | bytes 3145732
  210.7 111.6 %copy-start.4 = (bf16[512,512]{1,0:T(8,128)(2,1)S(1)}, bf16[512,512]{1,0:T(8,128)(2,1)}, u32[]{:S(2)}) copy-start(bf16[512,512]{1,0:T(8,128)(2,1)} %param.6) | copy-start | bytes 1572868
  210.7 111.6 %copy-start.9 = (f32[512]{0:T(512)S(1)}, f32[512]{0:T(512)}, u32[]{:S(2)}) copy-start(f32[512]{0:T(512)} %param.10) | copy-start | bytes 6148
  210.7 111.6 %all-gather.7.cloned.1.call-start = ((), (), s32[]{:S(2)}) async-start(), calls=%async_computation.4 | async-start | bytes 5242880 | tf_op jit(solution)/shard_map/all_gather | solution.py:20
  266.4 118.7 %all-gather.13.cloned.1.call-start = ((), (), s32[]{:S(2)}) async-start(), calls=%async_computation.9 | async-start | bytes 5242880 | tf_op jit(solution)/shard_map/all_gather | solution.py:20
  327.9 116.7 %copy-start.1 = (f32[512,512]{1,0:T(8,128)S(1)}, f32[512,512]{1,0:T(8,128)}, u32[]{:S(2)}) copy-start(f32[512,512]{1,0:T(8,128)} %fusion.12) | copy-start | bytes 3145732
  327.9 116.7 %all-gather.9.cloned.1.call-start = ((), (), s32[]{:S(2)}) async-start(), calls=%async_computation.5 | async-start | bytes 5242880 | tf_op jit(solution)/shard_map/all_gather | solution.py:20
  388.8 84.0 %reduce-scatter.3.cloned.1.call-start = ((), (), s32[]{:S(2)}) async-start(), calls=%async_computation.6 | async-start | bytes 3145728 | tf_op jit(solution)/shard_map/reduce_scatter | solution.py:35
  451.5 21.3 %copy-start.6 = (bf16[512,1024]{1,0:T(8,128)(2,1)S(1)}, bf16[512,1024]{1,0:T(8,128)(2,1)}, u32[]{:S(2)}) copy-start(bf16[512,1024]{1,0:T(8,128)(2,1)} %copy-done.5) | copy-start | bytes 3145732
  451.5 95.9 %reduce-scatter.5.cloned.1.call-start = ((), (), s32[]{:S(2)}) async-start(), calls=%async_computation.7 | async-start | bytes 1114112 | tf_op jit(solution)/shard_map/reduce_scatter | solution.py:35
Sparse Core Ops, SparseCore 0:
  10.9 46.7 all-reduce.2
  60.1 145.6 all-reduce.4
  210.8 51.9 all-gather.10
  266.6 55.6 all-gather.6
  328.0 57.0 all-gather.12
  388.9 55.6 all-gather.8
  451.6 21.1 reduce-scatter.2
  475.6 71.7 reduce-scatter.4
